TPU v7x, 512 devices: a whole 4x4x16 slice. The times are simulated.
512 devices in a mesh: grp: 4 (over x), gx: 128 (over z, y, core).
Axes of the slice: x: 4, y: 4, z: 16, core: 2. Of those that a mesh axis runs over, the one named last changes fastest.
Arguments:
- fourier: bfloat16 [128, 2, 16, 2560], P(None, None, 'grp', 'gx'), may hold values from -6 to 6
- lat_of_row: int32 [2560], replicated, may hold values from 0 to 2559, each once
- wave_order: int32 [128], replicated, may hold values from 0 to 127, each once
- analysis: bfloat16 [128, 128, 1280], P('gx'), may hold values from -0.125 to 0.125
- synthesis: bfloat16 [128, 1024, 128], P('gx'), may hold values from -0.046875 to 0.046875
- bracket: int32 [8, 1024, 3600], P(None, 'gx', 'grp'), may hold values from 0 to 14
- frac: float32 [8, 1024, 3600], P(None, 'gx', 'grp'), may hold values from 0 to 1
Outputs:
- pressure_field: float32 [8, 1024, 3600], P(None, 'gx', 'grp')
Inputs may be any that keep to these rules, and one draw needn't show every extreme that they name: `lat_of_row`: each latitude index appears once. `wave_order`: each window index appears once.
All inputs are finite; a program needn't handle non-finite values.
Results may differ from a plain program's by a relative error of at most 0.0046.
Values may be sent and summed in bfloat16 or wider, within the bound.
A program may use at most 64 MiB of HBM per device.

v0:
```python
import math

import jax
import jax.numpy as jnp
from jax import lax
from jax.sharding import PartitionSpec as P

MTOT = 1280


def inverse_table(wave_order, m_win, lon_start, count, n_lon):
    wave_m = MTOT - m_win + wave_order
    lons = lon_start + jnp.arange(count, dtype=jnp.int32)
    phase = wave_m[:, None] * lons[None, :] % n_lon
    angle = phase.astype(jnp.float32) * (2.0 * math.pi / n_lon)
    return jnp.stack([2.0 * jnp.cos(angle), -2.0 * jnp.sin(angle)], axis=1).astype(jnp.bfloat16)


def transform(piece, table):
    return jnp.einsum("celr,cen->lrn", piece, table, preferred_element_type=jnp.float32)


def shards(fourier, lat_of_row, wave_order, analysis, synthesis, bracket, frac):
    m_win = fourier.shape[0]
    rows_dev = fourier.shape[3]
    n_lat = lat_of_row.shape[0]
    m_dev = analysis.shape[0]
    half_lat = analysis.shape[2]
    lon_dev = bracket.shape[2]
    n_lon = lon_dev * lax.axis_size("grp")
    my_lats = lax.dynamic_slice_in_dim(lat_of_row, lax.axis_index("gx") * rows_dev, rows_dev, 0)
    pole = jnp.minimum(my_lats, n_lat - 1 - my_lats)
    loop_len = 20 + 4 * pole
    wave_m = MTOT - m_win + jnp.arange(m_win, dtype=jnp.int32)
    live = 2 * wave_m[:, None] < loop_len[None, :]
    masked = jnp.where(live[:, None, None, :], fourier, jnp.zeros((), fourier.dtype))
    ordered = jnp.take(masked, wave_order, axis=0)
    row_of_lat = (
        jnp.zeros((n_lat,), jnp.int32).at[lat_of_row].set(jnp.arange(n_lat, dtype=jnp.int32))
    )
    own_waves = lax.dynamic_slice_in_dim(wave_order, lax.axis_index("gx") * m_dev, m_dev, 0)
    degree = jnp.arange(m_win, dtype=jnp.int32)
    parity = jnp.where(degree % 2 == 0, 1.0, -1.0).astype(jnp.float32)
    keep = degree[None, :] < (m_win - own_waves)[:, None]
    loops = jnp.take(
        lax.all_to_all(ordered, "gx", split_axis=0, concat_axis=3, tiled=True), row_of_lat, axis=3
    )
    north = loops[..., :half_lat]
    south = jnp.flip(loops[..., half_lat:], axis=3)
    from_north = jnp.einsum("celj,ckj->celk", north, analysis, preferred_element_type=jnp.float32)
    from_south = jnp.einsum("celj,ckj->celk", south, analysis, preferred_element_type=jnp.float32)
    summed = from_north + parity * from_south
    spectra = jnp.where(keep[:, None, None, :], summed, 0.0).astype(jnp.bfloat16)
    grid_four = jnp.einsum(
        "celk,crk->celr", spectra, synthesis, preferred_element_type=jnp.float32
    ).astype(jnp.bfloat16)
    lon_start = lax.axis_index("grp") * lon_dev
    table = inverse_table(wave_order, m_win, lon_start, lon_dev, n_lon)
    back = lax.all_to_all(grid_four, "gx", split_axis=3, concat_axis=0, tiled=True)
    field = transform(lax.all_gather(back, "grp", axis=2, tiled=True), table)
    n_levels = field.shape[0]
    levels = jnp.arange(n_levels, dtype=jnp.int32)[:, None, None, None]
    chosen = bracket[None]
    weights = jnp.where(levels == chosen, 1.0 - frac[None], 0.0) + jnp.where(
        levels == chosen + 1, frac[None], 0.0
    )
    return jnp.sum(weights * field[:, None], axis=0)


def solution(mesh):
    placed = (
        P(None, None, "grp", "gx"),
        P(),
        P(),
        P("gx", None, None),
        P("gx", None, None),
        P(None, "gx", "grp"),
        P(None, "gx", "grp"),
    )
    return jax.shard_map(
        shards, mesh=mesh, in_specs=placed, out_specs=P(None, "gx", "grp"), check_vma=False
    )
```

profile of v0, /device:TPU:24, one launch (start us, length us, event | category | flops | bytes accessed | tf_op | source)
XLA Modules:
  0.0 115.0 jit_solution(14723292455756399718)
XLA Ops:
  0.0 0.0 copy-start
  0.0 0.0 copy-start.7
  0.0 0.0 copy-start.6
  0.0 0.0 copy-start.2
  0.0 0.7 compare_select_fusion.2
  0.8 0.7 compare_and_fusion.1
  1.4 0.0 copy-start.1
  1.4 0.8 fusion.25
  2.2 0.1 broadcast_compare_fusion
  2.3 0.8 broadcast_select_fusion.1
  3.1 0.2 copy.33
  3.4 0.8 gather_fusion
  4.2 0.9 broadcast_select_fusion
  5.1 19.3 %all-to-all-start = ((bf16[128,2,4,20]{3,2,1,0:T(4,128)(2,1)}), bf16[128,2,4,20]{3,2,1,0:T(4,128)(2,1)S(1)}, u32[]{:S(2)}, u32[]{:S(2)}) async-start(bf16[128,2,4,20]{3,2,1,0:T(4,128)(2,1)} %broadcast_select_fusion), calls=%async_computation | async-start | bytes 524288 | tf_op jit(solution)/shard_map/all_to_all | solution.py:46
  24.4 0.0 copy-done.6
  24.4 9.9 %scatter_custom_fusion = s32[2560]{0:T(1024)S(1)} fusion(s32[2560]{0:T(1024)S(1)} %compare_select_fusion.1, s32[2560]{0:T(1024)S(1)} %iota.28, s32[]{:T(128)} %constant.41.clone.1), kind=kCustom, calls=%fused_computation.42 | custom fusion | bytes 10244 | tf_op jit(solution)/shard_map/scatter | solution.py:39
  34.4 0.0 copy-done.7
  34.4 0.6 dynamic_slice.6
  35.1 0.0 copy-done.2
  35.1 0.7 broadcast_add_fusion
  35.8 0.0 copy-done.1
  35.8 0.7 broadcast_subtract_fusion
  37.2 9.1 %all-to-all-done = bf16[128,2,4,20]{3,2,1,0:T(4,128)(2,1)S(1)} async-done(((bf16[128,2,4,20]{3,2,1,0:T(4,128)(2,1)}), bf16[128,2,4,20]{3,2,1,0:T(4,128)(2,1)S(1)}, u32[]{:S(2)}, u32[]{:S(2)}) %all-to-all-start) | async-done | bytes 40992 | tf_op jit(solution)/shard_map/all_to_all | solution.py:46
  46.3 2.0 %copy.41 = bf16[1,2,4,128,20]{2,1,4,3,0:T(2,128)(2,1)S(1)} copy(bf16[1,2,4,128,20]{4,2,1,3,0:T(4,128)(2,1)S(1)} %bitcast.43) | data formatting | bytes 81920 | tf_op jit(solution)/shard_map/all_to_all | solution.py:46
  48.4 8.3 %gather_fusion.1 = bf16[2560,2,4]{2,1,0:T(2,128)(2,1)S(1)} fusion(bf16[2,4,2560]{1,0,2:T(2,128)(2,1)S(1)} %bitcast.42, s32[3072]{0:T(1024)S(1)} %pad_clamp_fusion), kind=kCustom, calls=%fused_computation.1 | custom fusion | bytes 92160 | tf_op jit(solution)/shard_map/jit(_take)/gather | solution.py:45
  56.7 0.0 copy-start.5
  56.7 0.9 copy.36
  57.7 0.9 rev.4
  58.6 0.0 copy-done
  58.6 0.2 fusion.13
  58.8 0.0 copy-done.5
  58.8 0.4 fusion
  59.2 1.2 %copy.37 = bf16[1,2,4,1024]{2,1,0,3:T(2,128)(2,1)} copy(bf16[1,2,4,1024]{3,2,1,0:T(4,128)(2,1)S(1)} %fusion) | data formatting | bytes 32768 | tf_op jit(solution)/shard_map/convert_element_type | solution.py:56
  60.4 7.0 %all-to-all-start.1 = ((bf16[1,2,4,1024]{2,1,0,3:T(2,128)(2,1)}), bf16[1,2,4,1024]{2,1,0,3:T(2,128)(2,1)S(1)}, u32[]{:S(2)}, u32[]{:S(2)}) async-start(bf16[1,2,4,1024]{2,1,0,3:T(2,128)(2,1)} %copy.37), calls=%async_computation.1 | async-start | bytes 1048576 | tf_op jit(solution)/shard_map/all_to_all | solution.py:59
  67.4 0.0 copy-start.3
  67.4 0.0 copy-start.4
  67.4 2.3 %multiply_convert_fusion.1 = (bf16[128,1,900]{0,2,1:T(8,128)(2,1)S(1)}, bf16[128,1,900]{0,2,1:T(8,128)(2,1)S(1)}) fusion(s32[900]{0:T(1024)S(1)} %iota_add_fusion, s32[128]{0:T(128)S(1)} %get-tuple-element.8), kind=kLoop, calls=%fused_computation.20 | loop fusion | flops 1497600 | bytes 464912 | tf_op jit(solution)/shard_map/convert
  69.7 30.7 %all-to-all-done.1 = bf16[1,2,4,1024]{2,1,0,3:T(2,128)(2,1)S(1)} async-done(((bf16[1,2,4,1024]{2,1,0,3:T(2,128)(2,1)}), bf16[1,2,4,1024]{2,1,0,3:T(2,128)(2,1)S(1)}, u32[]{:S(2)}, u32[]{:S(2)}) %all-to-all-start.1) | async-done | bytes 16416 | tf_op jit(solution)/shard_map/all_to_all | solution.py:59
  100.3 0.4 copy.43
  100.7 12.2 %all-gather = bf16[128,1,2,16,8]{0,4,2,1,3:T(8,128)(2,1)S(1)} all-gather(bf16[128,1,2,4,8]{0,4,2,1,3:T(8,128)(2,1)S(1)} %bitcast.44), channel_id=2, replica_groups=mesh['grp'=4,'gx'=128] {'grp'}, dimensions={3}, use_global_device_ids=true | all-gather | bytes 81920 | tf_op jit(solution)/shard_map/all_gather | solution.py:60
  112.9 0.3 convolution_bitcast_fusion
  113.2 0.0 copy-done.3
  113.3 0.0 copy-done.4
  113.3 1.7 %multiply_reduce_fusion = f32[8,8,900]{2,1,0:T(8,128)} fusion(f32[16,8,900]{2,1,0:T(8,128)S(1)} %convolution_bitcast_fusion, f32[8,8,900]{2,1,0:T(8,128)S(1)} %copy-done.1, s32[8,8,900]{2,1,0:T(8,128)S(1)} %copy-done.3, f32[8,8,900]{2,1,0:T(8,128)S(1)} %copy-done.4, s32[8,8,900]{2,1,0:T(8,128)S(1)} %copy-done.2), kind=kLoop, calls=%fused_computation.3 | loop fusion | flops 6393600 | bytes 1612800 | tf_op jit(solution)/shard_map/reduce_sum | solution.py:67
  (12 shorter events, 0.1 us)
Async XLA Ops:
  0.0 58.6 %copy-start = (bf16[1,128,1280]{2,1,0:T(8,128)(2,1)S(1)}, bf16[1,128,1280]{2,1,0:T(8,128)(2,1)}, u32[]{:S(2)}) copy-start(bf16[1,128,1280]{2,1,0:T(8,128)(2,1)} %param.10) | copy-start | bytes 983044
  0.0 34.4 %copy-start.7 = (s32[128]{0:T(128)S(1)}, s32[128]{0:T(128)}, u32[]{:S(2)}) copy-start(s32[128]{0:T(128)} %param.9) | copy-start | bytes 1540
  0.0 24.4 %copy-start.6 = (s32[2560]{0:T(1024)S(1)}, s32[2560]{0:T(1024)}, u32[]{:S(2)}) copy-start(s32[2560]{0:T(1024)} %param.8) | copy-start | bytes 30724
  0.0 35.1 %copy-start.2 = (s32[8,8,900]{2,1,0:T(8,128)S(1)}, s32[8,8,900]{2,1,0:T(8,128)}, u32[]{:S(2)}) copy-start(s32[8,8,900]{2,1,0:T(8,128)} %param.12) | copy-start | bytes 691204
  1.4 34.4 %copy-start.1 = (f32[8,8,900]{2,1,0:T(8,128)S(1)}, f32[8,8,900]{2,1,0:T(8,128)}, u32[]{:S(2)}) copy-start(f32[8,8,900]{2,1,0:T(8,128)} %param.13) | copy-start | bytes 691204
  5.1 41.2 %all-to-all-start = ((bf16[128,2,4,20]{3,2,1,0:T(4,128)(2,1)}), bf16[128,2,4,20]{3,2,1,0:T(4,128)(2,1)S(1)}, u32[]{:S(2)}, u32[]{:S(2)}) async-start(bf16[128,2,4,20]{3,2,1,0:T(4,128)(2,1)} %broadcast_select_fusion), calls=%async_computation | async-start | bytes 524288 | tf_op jit(solution)/shard_map/all_to_all | solution.py:46
  56.7 2.1 %copy-start.5 = (bf16[1,1024,128]{2,1,0:T(8,128)(2,1)S(1)}, bf16[1,1024,128]{2,1,0:T(8,128)(2,1)}, u32[]{:S(2)}) copy-start(bf16[1,1024,128]{2,1,0:T(8,128)(2,1)} %param.11) | copy-start | bytes 786436
  60.4 40.0 %all-to-all-start.1 = ((bf16[1,2,4,1024]{2,1,0,3:T(2,128)(2,1)}), bf16[1,2,4,1024]{2,1,0,3:T(2,128)(2,1)S(1)}, u32[]{:S(2)}, u32[]{:S(2)}) async-start(bf16[1,2,4,1024]{2,1,0,3:T(2,128)(2,1)} %copy.37), calls=%async_computation.1 | async-start | bytes 1048576 | tf_op jit(solution)/shard_map/all_to_all | solution.py:59
  67.4 45.9 %copy-start.3 = (s32[8,8,900]{2,1,0:T(8,128)S(1)}, s32[8,8,900]{2,1,0:T(8,128)}, u32[]{:S(2)}) copy-start(s32[8,8,900]{2,1,0:T(8,128)} %broadcast_add_fusion) | copy-start | bytes 691204
  67.4 45.9 %copy-start.4 = (f32[8,8,900]{2,1,0:T(8,128)S(1)}, f32[8,8,900]{2,1,0:T(8,128)}, u32[]{:S(2)}) copy-start(f32[8,8,900]{2,1,0:T(8,128)} %broadcast_subtract_fusion) | copy-start | bytes 691204
where the time goes:
time: 115 us
  waiting for transfers between devices  39.8 us (35%)
  starting transfers between devices  26.3 us (23%)
  local copies, waits for them, and re-layouts  25.4 us (22%)
  blocking collectives  12.2 us (11%)
  other arithmetic  9.48 us (8%)
    all_to_all x1, waiting for transfers between devices, shards(): lax.all_to_all(grid_four, 'gx', split_axis=3, concat_axis=0, tiled=True)  30.7 us
    all_to_all x1, starting transfers between devices, shards(): lax.all_to_all(ordered, 'gx', split_axis=0, concat_axis=3, tiled=True)  19.3 us
    all_gather x1, blocking collectives, shards(): field = transform(lax.all_gather(back, 'grp', axis=2, tiled=True), table)  12.2 us
    scatter x1, local copies, waits for them, and re-layouts, shards(): jnp.zeros((n_lat,), jnp.int32).at[lat_of_row]  9.93 us
    gather x2, local copies, waits for them, and re-layouts, shards(): jnp.take(lax.all_to_all(ordered, 'gx', split_axis=0, concat_axis=3, tiled...  9.21 us
    all_to_all x1, waiting for transfers between devices, shards(): lax.all_to_all(ordered, 'gx', split_axis=0, concat_axis=3, tiled=True)  9.13 us
    all_to_all x1, starting transfers between devices, shards(): lax.all_to_all(grid_four, 'gx', split_axis=3, concat_axis=0, tiled=True)  7 us
  transfers between devices with their start and end apart: 2, of which 2 were waited for; matrix products, arithmetic and copies ran while one was open for 12% of the time, Pallas kernels for 0%

commit v1 on v0

v1 whole, which is shorter than its diff:
```python
import functools
import math

import jax
import jax.numpy as jnp
from jax import lax
from jax.experimental import pallas as pl
from jax.experimental.pallas import tpu as pltpu
from jax.sharding import PartitionSpec as P

MESH = pl.DeviceIdType.MESH
F32, BF16, I32 = jnp.float32, jnp.bfloat16, jnp.int32

NX, NZ, NYC = 4, 16, 8
NGX = NZ * NYC
MTOT, NLAT, NLON = 1280, 2560, 3600
WAVES = 128
FIRST_WAVE = MTOT - WAVES
LEV_DEV, ROWS_DEV, LOOPS_DEV, LON_DEV, POUT, LEV = 4, 8, 20, 900, 8, 16
HALF = NLAT // 2
LANES = 128
LON_PAD = 1024


def iota(shape, axis):
    return lax.broadcasted_iota(I32, shape, axis)


def nt_dot(a, b):
    return lax.dot_general(a, b, (((1,), (1,)), ((), ())), preferred_element_type=F32)


def nn_dot(a, b):
    return lax.dot_general(a, b, (((1,), (0,)), ((), ())), preferred_element_type=F32)


def slot_source(shape):
    lane = iota(shape, 1)
    return (lane & (NZ - 1)) * NYC + (lane >> 4)


def ordered_waves(fourier, wave):
    pick = (iota((WAVES, WAVES), 0) == wave).astype(F32)
    pick = pick.T.astype(BF16)
    rows = jnp.concatenate([fourier[0].astype(F32), fourier[1].astype(F32)], axis=1)
    rows = rows.reshape(LOOPS_DEV * 8, WAVES)
    rows = jnp.concatenate([rows, jnp.zeros((256 - LOOPS_DEV * 8, WAVES), F32)], axis=0)
    return nt_dot(pick, rows.astype(BF16))


def loop_lats(lat):
    flat = slot_source((24, LANES)) * LOOPS_DEV + jnp.minimum(iota((24, LANES), 0), LOOPS_DEV - 1)
    high, low = flat >> 7, flat & (LANES - 1)
    out = jnp.zeros((24, LANES), I32)
    for a in range(LOOPS_DEV):
        row = jnp.broadcast_to(lat[a : a + 1], (24, LANES))
        out = jnp.where(high == a, jnp.take_along_axis(row, low, axis=1), out)
    return out


def table_tile(wave_col, lon):
    turns = wave_col * lon
    quarter = jnp.floor(turns.astype(F32) * (4.0 / NLON) + 0.5).astype(I32)
    rest = (turns - quarter * (NLON // 4)).astype(F32) * (2.0 * math.pi / NLON)
    sq = rest * rest
    c = 1.0 + sq * (-0.5 + sq * (1.0 / 24 + sq * (-1.0 / 720 + sq * (1.0 / 40320))))
    s = rest * (1.0 + sq * (-1.0 / 6 + sq * (1.0 / 120 + sq * (-1.0 / 5040 + sq * (1.0 / 362880)))))
    odd = (quarter & 1) == 1
    cos = jnp.where(odd, s, c)
    sin = jnp.where(odd, c, s)
    cos = jnp.where(((quarter + 1) & 2) == 2, -2.0 * cos, 2.0 * cos)
    sin = jnp.where((quarter & 2) == 2, 2.0 * sin, -2.0 * sin)
    return cos.astype(BF16), sin.astype(BF16)


def kernel(
    lat_ref, wave_ref, fourier_ref, analysis_ref, synthesis_ref, bracket_ref, frac_ref,
    out_ref,
    fourier_v, analysis_v, synthesis_v, bracket_v, frac_v,
    send1, recv1, send2, recv2, send3, recv3, send4, recv4,
    lats_s, sorted_s, spread_s, rows_s, syn_f, syn_s, wave_s, table_s, field_s,
    local_sem, send_sem, recv_sem,
):
    x = lax.axis_index("grp")
    gx = lax.axis_index("gx")
    z, yc = lax.div(gx, NYC), lax.rem(gx, NYC)

    local = [
        pltpu.make_async_copy(src, dst, local_sem.at[i])
        for i, (src, dst) in enumerate(
            (
                (fourier_ref, fourier_v),
                (analysis_ref, analysis_v),
                (synthesis_ref, synthesis_v),
                (bracket_ref, bracket_v),
                (frac_ref, frac_v),
            )
        )
    ]
    for copy in local:
        copy.start()

    barrier = pltpu.get_barrier_semaphore()

    @pl.loop(1, NZ)
    def _(d):
        pl.semaphore_signal(
            barrier, inc=1, device_id=(x, lax.rem(z + d, NZ) * NYC + yc), device_id_type=MESH
        )

    @pl.loop(1, NX * NYC)
    def _(d):
        tx = lax.rem(x + lax.div(d, NYC), NX)
        ty = lax.rem(yc + lax.rem(d, NYC), NYC)
        pl.semaphore_signal(barrier, inc=1, device_id=(tx, z * NYC + ty), device_id_type=MESH)

    def exchange_z(send, recv, stage):
        pltpu.make_async_copy(send.at[z], recv.at[z], recv_sem.at[stage]).start()

        @pl.loop(1, NZ)
        def _(d):
            tz = lax.rem(z + d, NZ)
            pltpu.make_async_remote_copy(
                src_ref=send.at[tz],
                dst_ref=recv.at[z],
                send_sem=send_sem.at[stage],
                recv_sem=recv_sem.at[stage],
                device_id=(x, tz * NYC + yc),
                device_id_type=MESH,
            ).start()

    def wait_all(ref, sem):
        pltpu.make_async_copy(ref, ref, sem).wait()

    wave = wave_ref[...]
    local[0].wait()
    ordered = ordered_waves(fourier_v[...], wave)
    head = ordered[:, :LANES].reshape(NZ, NYC, LANES)
    tail = ordered[:, LANES:].reshape(NZ, NYC, LANES)
    send1[...] = jnp.concatenate([head, tail], axis=1).astype(BF16)
    pl.semaphore_wait(barrier, NZ - 1 + NX * NYC - 1)
    exchange_z(send1, recv1, 0)

    lats = loop_lats(lat_ref[...])
    own = jnp.sum(jnp.where(iota((1, WAVES), 1) == gx, wave, 0), axis=1, keepdims=True)
    pole = jnp.minimum(lats, NLAT - 1 - lats)
    live = 2 * (FIRST_WAVE + own) < 20 + 4 * pole
    lats_s[0] = jnp.where(live, pole, -1)
    lats_s[1] = jnp.where(lats >= HALF, 1, 0)
    local[1].wait()

    def sort_pair(pair):
        row = lats_s[0, pl.ds(2 * pair, 2), :]
        south = lats_s[1, pl.ds(2 * pair, 2), :]
        row = jnp.concatenate([row[0:1], row[1:2]], axis=1)
        south = jnp.concatenate([south[0:1], south[1:2]], axis=1)
        total = jnp.zeros((WAVES, 2 * LANES), F32)
        for j in range(0, HALF, 256):
            hot = (iota((256, 2 * LANES), 0) + j == row).astype(F32).astype(BF16)
            total += nn_dot(analysis_v[:, j : j + 256], hot)
        odd = iota((WAVES, 2 * LANES), 0) & 1
        total = jnp.where((odd * south) == 1, -total, total)
        sorted_s[:, pl.ds(pl.multiple_of(pair * 256, 256), 256)] = total.astype(BF16)

    pl.loop(0, LOOPS_DEV // 4)(sort_pair)

    wait_all(recv1, recv_sem.at[0])
    spread_s[...] = recv1[...].astype(F32).reshape(NZ * 16, LANES)
    for ty in range(NYC):
        send2[ty, :, :LANES] = spread_s[pl.ds(ty, NZ, stride=16), :].astype(BF16)
        send2[ty, :, LANES:] = spread_s[pl.ds(8 + ty, NZ, stride=16), :].astype(BF16)
    pltpu.make_async_copy(send2.at[yc], recv2.at[yc], recv_sem.at[1]).start()

    @pl.loop(1, NYC)
    def _(d):
        ty = lax.rem(yc + d, NYC)
        pltpu.make_async_remote_copy(
            src_ref=send2.at[ty],
            dst_ref=recv2.at[yc],
            send_sem=send_sem.at[1],
            recv_sem=recv_sem.at[1],
            device_id=(x, z * NYC + ty),
            device_id_type=MESH,
        ).start()

    pl.loop(LOOPS_DEV // 4, LOOPS_DEV // 2)(sort_pair)
    local[2].wait()
    syn_f[...] = synthesis_v[...].astype(F32)
    for ri in range(ROWS_DEV):
        syn_s[:, ri * LANES : (ri + 1) * LANES] = syn_f[pl.ds(ri, NGX, stride=ROWS_DEV), :].astype(BF16)

    wait_all(recv2, recv_sem.at[1])
    loops = recv2[...].reshape(NGX, 2 * LANES).astype(F32)
    loops = jnp.concatenate([loops[:, :LANES].T, loops[:, LANES:].T], axis=0)
    loops = jnp.concatenate([loops[8 * s : 8 * s + 8] for s in range(LOOPS_DEV)], axis=1)
    spec = nt_dot(loops.astype(BF16), sorted_s[...])
    spec = jnp.where(iota((8, WAVES), 1) < WAVES - own, spec, 0.0).astype(BF16).astype(F32)
    wide = jnp.broadcast_to(spec[:, None, :], (8, ROWS_DEV, WAVES)).reshape(8 * ROWS_DEV, WAVES)
    ri = iota((8 * ROWS_DEV, WAVES), 0) & (ROWS_DEV - 1)
    wide = jnp.concatenate([jnp.where(ri == r, wide, 0.0) for r in range(ROWS_DEV)], axis=1)
    wide = jnp.concatenate([wide, jnp.zeros_like(wide)], axis=0).astype(BF16)
    rows = nt_dot(syn_s[...], wide)
    send3[...] = rows.reshape(NZ, NYC, LANES).astype(BF16)

    exchange_z(send3, recv3, 2)
    lane = iota((1, WAVES), 1)
    source = jnp.broadcast_to((lane & (NZ - 1)) * NYC + (lane >> 4), (8, WAVES))
    waves = jnp.take_along_axis(jnp.broadcast_to(wave, (8, WAVES)), source, axis=1)
    waves = jnp.broadcast_to(waves[0:1].astype(F32), (WAVES, WAVES)).T
    wave_s[...] = waves.astype(I32) + FIRST_WAVE
    lon_start = x * LON_DEV

    def table_rows(i):
        at = pl.ds(pl.multiple_of(i * 16, 16), 16)
        col = wave_s[at, :]
        for n in range(0, LON_PAD, LANES):
            lon = iota((16, LANES), 1) + (lon_start + n)
            cos, sin = table_tile(col, lon)
            table_s[0, at, n : n + LANES] = cos
            table_s[1, at, n : n + LANES] = sin

    pl.loop(0, 4)(table_rows)

    wait_all(recv3, recv_sem.at[2])
    rows_s[...] = recv3[...].astype(F32).reshape(NGX, LANES)
    for ty in range(NYC):
        send4[ty] = rows_s[pl.ds(ty, NZ, stride=NYC), :].astype(BF16)
    pltpu.make_async_copy(send4.at[yc], recv4.at[x, yc], recv_sem.at[3]).start()

    @pl.loop(1, NX * NYC)
    def _(d):
        tx = lax.rem(x + lax.div(d, NYC), NX)
        ty = lax.rem(yc + lax.rem(d, NYC), NYC)
        pltpu.make_async_remote_copy(
            src_ref=send4.at[ty],
            dst_ref=recv4.at[x, yc],
            send_sem=send_sem.at[3],
            recv_sem=recv_sem.at[3],
            device_id=(tx, z * NYC + ty),
            device_id_type=MESH,
        ).start()

    pl.loop(4, 8)(table_rows)

    wait_all(recv4, recv_sem.at[3])
    parts = []
    for tx in range(NX):
        block = recv4[tx].reshape(NGX, LANES).astype(F32).T
        parts.append(jnp.concatenate([block[0:32], block[32:64]], axis=1))
    rows = jnp.concatenate(parts, axis=0).astype(BF16)
    field = nn_dot(rows, table_s[...].reshape(2 * NGX, LON_PAD))
    field_s[...] = field.reshape(LEV, ROWS_DEV, LON_PAD)
    local[3].wait()
    local[4].wait()

    for n in range(0, LON_DEV, LANES):
        at = slice(n, min(n + LANES, LON_DEV))
        levels = [field_s[v, :, at] for v in range(LEV)]

        @pl.loop(0, POUT)
        def _(p):
            below = bracket_v[p, :, at]
            weight = frac_v[p, :, at]
            low, high = levels, levels[1:] + levels[-1:]
            for bit in range(4):
                mask = ((below >> bit) & 1) == 1
                low = [jnp.where(mask, b, a) for a, b in zip(low[0::2], low[1::2])]
                high = [jnp.where(mask, b, a) for a, b in zip(high[0::2], high[1::2])]
            out_ref[p, :, at] = (1.0 - weight) * low[0] + weight * high[0]

    wait_all(send1.at[pl.ds(0, NZ - 1)], send_sem.at[0])
    wait_all(send2.at[pl.ds(0, NYC - 1)], send_sem.at[1])
    wait_all(send3.at[pl.ds(0, NZ - 1)], send_sem.at[2])
    wait_all(recv4.at[pl.ds(0, NX - 1)], send_sem.at[3])
    wait_all(recv4.at[0, pl.ds(0, NYC - 1)], send_sem.at[3])


def shards(fourier, lat_of_row, wave_order, analysis, synthesis, bracket, frac):
    lat = lat_of_row.reshape(LOOPS_DEV, LANES)
    wave = wave_order.reshape(1, WAVES)
    fourier = jnp.transpose(fourier, (1, 3, 2, 0))
    vmem = pl.BlockSpec(memory_space=pltpu.VMEM)
    hbm = pl.BlockSpec(memory_space=pl.ANY)
    return pl.pallas_call(
        kernel,
        out_shape=jax.ShapeDtypeStruct((POUT, ROWS_DEV, LON_DEV), F32),
        in_specs=[vmem, vmem, hbm, hbm, hbm, hbm, hbm],
        out_specs=vmem,
        scratch_shapes=[
            pltpu.VMEM((2, LOOPS_DEV, LEV_DEV, WAVES), BF16),
            pltpu.VMEM((WAVES, HALF), BF16),
            pltpu.VMEM((NGX * ROWS_DEV, WAVES), BF16),
            pltpu.VMEM((POUT, ROWS_DEV, LON_DEV), I32),
            pltpu.VMEM((POUT, ROWS_DEV, LON_DEV), F32),
            pltpu.VMEM((NZ, 16, LANES), BF16),
            pltpu.VMEM((NZ, 16, LANES), BF16),
            pltpu.VMEM((NYC, NZ, 2 * LANES), BF16),
            pltpu.VMEM((NYC, NZ, 2 * LANES), BF16),
            pltpu.VMEM((NZ, NYC, LANES), BF16),
            pltpu.VMEM((NZ, NYC, LANES), BF16),
            pltpu.VMEM((NYC, NZ, LANES), BF16),
            pltpu.VMEM((NX, NYC, NZ, LANES), BF16),
            pltpu.VMEM((2, 24, LANES), I32),
            pltpu.VMEM((WAVES, NLAT), BF16),
            pltpu.VMEM((NZ * 16, LANES), F32),
            pltpu.VMEM((NGX, LANES), F32),
            pltpu.VMEM((NGX * ROWS_DEV, WAVES), F32),
            pltpu.VMEM((NGX, ROWS_DEV * WAVES), BF16),
            pltpu.VMEM((WAVES, LANES), I32),
            pltpu.VMEM((2, NGX, LON_PAD), BF16),
            pltpu.VMEM((LEV, ROWS_DEV, LON_PAD), F32),
            pltpu.SemaphoreType.DMA((5,)),
            pltpu.SemaphoreType.DMA((4,)),
            pltpu.SemaphoreType.DMA((4,)),
        ],
        compiler_params=pltpu.CompilerParams(
            collective_id=0, has_side_effects=True, vmem_limit_bytes=32 * 1024 * 1024
        ),
        cost_estimate=pl.CostEstimate(flops=10**9, bytes_accessed=1400000, transcendentals=0),
    )(
        lat, wave, fourier, analysis.reshape(WAVES, HALF),
        synthesis.reshape(NGX * ROWS_DEV, WAVES), bracket, frac,
    )


def solution(mesh):
    placed = (
        P(None, None, "grp", "gx"),
        P(),
        P(),
        P("gx", None, None),
        P("gx", None, None),
        P(None, "gx", "grp"),
        P(None, "gx", "grp"),
    )
    return jax.shard_map(
        shards, mesh=mesh, in_specs=placed, out_specs=P(None, "gx", "grp"), check_vma=False
    )
```

time: 115 us -> 52 us (0.45)
  the two profiles are of different devices: /device:TPU:24 before, /device:TPU:1 now
where the time goes in v1:
time: 52 us; the launch traced here: 51.6 us
  Pallas kernels  45 us (87%)
  local copies, waits for them, and re-layouts  6.66 us (13%)
    pallas_call x1, Pallas kernels, shards(): pl.pallas_call(kernel, out_shape=jax.ShapeDtypeStruct((POUT, ROWS_DEV, LO...  45 us
    unnamed x15, local copies, waits for them, and re-layouts  6.66 us

profile of v1, /device:TPU:1, one launch (start us, length us, event | category | flops | bytes accessed | tf_op | source)
XLA Modules:
  0.0 51.6 jit_solution(116605255648162733)
XLA Ops:
  0.0 0.0 copy-start.6
  0.0 0.7 %copy-done.6 = s32[128]{0:T(128)S(1)} copy-done((s32[128]{0:T(128)S(1)}, s32[128]{0:T(128)}, u32[]{:S(2)}) %copy-start.6) | copy-done | bytes 536
  0.7 0.0 copy-start
  0.7 1.0 %copy-done = bf16[1,128,1280]{2,1,0:T(8,128)(2,1)S(1)} copy-done((bf16[1,128,1280]{2,1,0:T(8,128)(2,1)S(1)}, bf16[1,128,1280]{2,1,0:T(8,128)(2,1)}, u32[]{:S(2)}) %copy-start) | copy-done | bytes 327704
  1.6 0.0 copy-start.1
  1.6 0.9 %copy-done.1 = bf16[1,1024,128]{2,1,0:T(8,128)(2,1)S(1)} copy-done((bf16[1,1024,128]{2,1,0:T(8,128)(2,1)S(1)}, bf16[1,1024,128]{2,1,0:T(8,128)(2,1)}, u32[]{:S(2)}) %copy-start.1) | copy-done | bytes 262168
  2.6 0.0 copy-start.2
  2.6 0.9 %copy-done.2 = s32[8,8,900]{2,1,0:T(8,128)S(1)} copy-done((s32[8,8,900]{2,1,0:T(8,128)S(1)}, s32[8,8,900]{2,1,0:T(8,128)}, u32[]{:S(2)}) %copy-start.2) | copy-done | bytes 230424
  3.5 0.0 copy-start.3
  3.5 0.9 %copy-done.3 = f32[8,8,900]{2,1,0:T(8,128)S(1)} copy-done((f32[8,8,900]{2,1,0:T(8,128)S(1)}, f32[8,8,900]{2,1,0:T(8,128)}, u32[]{:S(2)}) %copy-start.3) | copy-done | bytes 230424
  4.5 0.0 copy-start.4
  4.5 0.8 %copy-done.4 = bf16[128,2,4,20]{0,2,3,1:T(4,128)(2,1)S(1)} copy-done((bf16[128,2,4,20]{0,2,3,1:T(4,128)(2,1)S(1)}, bf16[128,2,4,20]{0,2,3,1:T(4,128)(2,1)}, u32[]{:S(2)}) %copy-start.4) | copy-done | bytes 40984
  5.3 0.0 copy-start.5
  5.3 0.7 %copy-done.5 = s32[2560]{0:T(1024)S(1)} copy-done((s32[2560]{0:T(1024)S(1)}, s32[2560]{0:T(1024)}, u32[]{:S(2)}) %copy-start.5) | copy-done | bytes 10264
  6.0 45.0 %shard_map.73 = f32[8,8,900]{2,1,0:T(8,128)S(1)} custom-call(s32[20,128]{1,0:T(8,128)S(1)} %bitcast.8, s32[1,128]{1,0:T(1,128)S(1)} %bitcast.9, bf16[2,20,4,128]{3,2,1,0:T(4,128)(2,1)S(1)} %bitcast.7, bf16[128,1280]{1,0:T(8,128)(2,1)S(1)} %bitcast.5, bf16[1024,128]{1,0:T(8,128)(2,1)S(1)} %bitcast.6, s32[8,8,900]{2,1,0:T(8,128)S(1)} %copy-done.2, ...), custom_call_target="tpu_custom_call" | custom-call | flops 1000000000 | bytes 1400000 | tf_op jit(solution)/shard_map/pallas_call | solution.py:284
  50.9 0.7 %copy.9 = f32[8,8,900]{2,1,0:T(8,128)} copy(f32[8,8,900]{2,1,0:T(8,128)S(1)} %shard_map.73) | data formatting | bytes 460800
Async XLA Ops:
  0.0 0.7 %copy-start.6 = (s32[128]{0:T(128)S(1)}, s32[128]{0:T(128)}, u32[]{:S(2)}) copy-start(s32[128]{0:T(128)} %param.9) | copy-start | bytes 1540
  0.7 1.0 %copy-start = (bf16[1,128,1280]{2,1,0:T(8,128)(2,1)S(1)}, bf16[1,128,1280]{2,1,0:T(8,128)(2,1)}, u32[]{:S(2)}) copy-start(bf16[1,128,1280]{2,1,0:T(8,128)(2,1)} %param.10) | copy-start | bytes 983044
  1.6 0.9 %copy-start.1 = (bf16[1,1024,128]{2,1,0:T(8,128)(2,1)S(1)}, bf16[1,1024,128]{2,1,0:T(8,128)(2,1)}, u32[]{:S(2)}) copy-start(bf16[1,1024,128]{2,1,0:T(8,128)(2,1)} %param.11) | copy-start | bytes 786436
  2.6 0.9 %copy-start.2 = (s32[8,8,900]{2,1,0:T(8,128)S(1)}, s32[8,8,900]{2,1,0:T(8,128)}, u32[]{:S(2)}) copy-start(s32[8,8,900]{2,1,0:T(8,128)} %bracket_ref.1) | copy-start | bytes 691204
  3.5 0.9 %copy-start.3 = (f32[8,8,900]{2,1,0:T(8,128)S(1)}, f32[8,8,900]{2,1,0:T(8,128)}, u32[]{:S(2)}) copy-start(f32[8,8,900]{2,1,0:T(8,128)} %frac_ref.1) | copy-start | bytes 691204
  4.5 0.8 %copy-start.4 = (bf16[128,2,4,20]{0,2,3,1:T(4,128)(2,1)S(1)}, bf16[128,2,4,20]{0,2,3,1:T(4,128)(2,1)}, u32[]{:S(2)}) copy-start(bf16[128,2,4,20]{0,2,3,1:T(4,128)(2,1)} %param.7) | copy-start | bytes 122884
  5.3 0.7 %copy-start.5 = (s32[2560]{0:T(1024)S(1)}, s32[2560]{0:T(1024)}, u32[]{:S(2)}) copy-start(s32[2560]{0:T(1024)} %param.8) | copy-start | bytes 30724

commit v2 on v1

v2 whole, which is shorter than its diff:
```python
import functools
import math

import jax
import jax.numpy as jnp
from jax import lax
from jax.experimental import pallas as pl
from jax.experimental.pallas import tpu as pltpu
from jax.sharding import PartitionSpec as P

MESH = pl.DeviceIdType.MESH
F32, BF16, I32 = jnp.float32, jnp.bfloat16, jnp.int32

NX, NZ, NYC = 4, 16, 8
NGX = NZ * NYC
MTOT, NLAT, NLON = 1280, 2560, 3600
WAVES = 128
FIRST_WAVE = MTOT - WAVES
LEV_DEV, ROWS_DEV, LOOPS_DEV, LON_DEV, POUT, LEV = 4, 8, 20, 900, 8, 16
HALF = NLAT // 2
LANES = 128
LON_PAD = 1024


def iota(shape, axis):
    return lax.broadcasted_iota(I32, shape, axis)


def nt_dot(a, b):
    return lax.dot_general(a, b, (((1,), (1,)), ((), ())), preferred_element_type=F32)


def nn_dot(a, b):
    return lax.dot_general(a, b, (((1,), (0,)), ((), ())), preferred_element_type=F32)


def ordered_waves(fourier, wave):
    pick = (iota((WAVES, WAVES), 0) == wave).astype(F32)
    pick = pick.T.astype(BF16)
    rows = jnp.concatenate([fourier[0].astype(F32), fourier[1].astype(F32)], axis=1)
    rows = rows.reshape(LOOPS_DEV * 8, WAVES)
    rows = jnp.concatenate([rows, jnp.zeros((256 - LOOPS_DEV * 8, WAVES), F32)], axis=0)
    return nt_dot(pick, rows.astype(BF16))


def loop_lats(lat):
    flat = iota((24, LANES), 1) * LOOPS_DEV + jnp.minimum(iota((24, LANES), 0), LOOPS_DEV - 1)
    high, low = flat >> 7, flat & (LANES - 1)
    out = jnp.zeros((24, LANES), I32)
    for a in range(LOOPS_DEV):
        row = jnp.broadcast_to(lat[a : a + 1], (24, LANES))
        out = jnp.where(high == a, jnp.take_along_axis(row, low, axis=1), out)
    return out


def table_tile(wave_col, lon):
    turns = wave_col * lon
    quarter = jnp.floor(turns.astype(F32) * (4.0 / NLON) + 0.5).astype(I32)
    rest = (turns - quarter * (NLON // 4)).astype(F32) * (2.0 * math.pi / NLON)
    sq = rest * rest
    c = 1.0 + sq * (-0.5 + sq * (1.0 / 24 + sq * (-1.0 / 720 + sq * (1.0 / 40320))))
    s = rest * (1.0 + sq * (-1.0 / 6 + sq * (1.0 / 120 + sq * (-1.0 / 5040 + sq * (1.0 / 362880)))))
    odd = (quarter & 1) == 1
    cos = jnp.where(odd, s, c)
    sin = jnp.where(odd, c, s)
    cos = jnp.where(((quarter + 1) & 2) == 2, -2.0 * cos, 2.0 * cos)
    sin = jnp.where((quarter & 2) == 2, 2.0 * sin, -2.0 * sin)
    return cos.astype(BF16), sin.astype(BF16)


def farthest_first(step, half):
    return half + ((step + 1) >> 1) * (1 - 2 * (step & 1))


def kernel(
    fourier_ref, wave_ref, lat_ref, analysis_ref, synthesis_ref, bracket_ref, frac_ref,
    out_ref,
    fourier_v, wave_v, lat_v, analysis_v, synthesis_v, bracket_v, frac_v,
    send1, recv1, send2, recv2, send3, recv3,
    lats_s, sorted_s, spread_s, syn_f, syn_s, wave_s, table_s, field_s,
    local_sem, send_sem, recv_sem,
):
    x = lax.axis_index("grp")
    gx = lax.axis_index("gx")
    z, yc = gx >> 3, gx & (NYC - 1)

    def peers(action):
        def near(tz, count):
            for j in range(count):
                action((tz << 3) + ((yc + farthest_first(j, NYC // 2)) & (NYC - 1)))

        @pl.loop(0, NZ - 1)
        def _(k):
            near((z + farthest_first(k, NZ // 2)) & (NZ - 1), NYC)

        near(z, NYC - 1)

    barrier = pltpu.get_barrier_semaphore()

    def signal(tx, to):
        pl.semaphore_signal(barrier, inc=1, device_id=(tx, to), device_id_type=MESH)

    peers(lambda to: signal(x, to))
    for d in (2, 1, 3):
        signal((x + d) & (NX - 1), gx)

    local = [
        pltpu.make_async_copy(src, dst, local_sem.at[i])
        for i, (src, dst) in enumerate(
            (
                (fourier_ref, fourier_v),
                (wave_ref, wave_v),
                (lat_ref, lat_v),
                (analysis_ref, analysis_v),
                (synthesis_ref, synthesis_v),
                (bracket_ref, bracket_v),
                (frac_ref, frac_v),
            )
        )
    ]
    for copy in local:
        copy.start()

    def exchange(send, recv, stage):
        def one(to):
            pltpu.make_async_remote_copy(
                src_ref=send(to),
                dst_ref=recv(gx),
                send_sem=send_sem.at[stage],
                recv_sem=recv_sem.at[stage],
                device_id=(x, to),
                device_id_type=MESH,
            ).start()

        peers(one)
        pltpu.make_async_copy(send(gx), recv(gx), recv_sem.at[stage]).start()

    def wait_all(ref, sem):
        pltpu.make_async_copy(ref, ref, sem).wait()

    local[0].wait()
    local[1].wait()
    wave = wave_v[...]
    ordered = ordered_waves(fourier_v[...], wave)
    spread_s[pl.ds(0, NGX, stride=2), :] = ordered[:, :LANES]
    spread_s[pl.ds(1, NGX, stride=2), :] = ordered[:, LANES:]
    send1.reshape(2 * NGX, LANES)[...] = spread_s[...].astype(BF16)
    pl.semaphore_wait(barrier, NGX - 1 + NX - 1)
    exchange(lambda to: send1.at[to], lambda to: recv1.at[to], 0)

    local[2].wait()
    lats = loop_lats(lat_v[...])
    own = jnp.sum(jnp.where(iota((1, WAVES), 1) == gx, wave, 0), axis=1, keepdims=True)
    pole = jnp.minimum(lats, NLAT - 1 - lats)
    live = 2 * (FIRST_WAVE + own) < 20 + 4 * pole
    lats_s[0] = jnp.where(live, pole, -1)
    lats_s[1] = jnp.where(lats >= HALF, 1, 0)
    local[3].wait()

    @pl.loop(0, LOOPS_DEV // 2)
    def _(pair):
        row = lats_s[0, pl.ds(2 * pair, 2), :]
        south = lats_s[1, pl.ds(2 * pair, 2), :]
        row = jnp.concatenate([row[0:1], row[1:2]], axis=1)
        south = jnp.concatenate([south[0:1], south[1:2]], axis=1)
        total = jnp.zeros((WAVES, 2 * LANES), F32)
        for j in range(0, HALF, 256):
            hot = (iota((256, 2 * LANES), 0) + j == row).astype(F32).astype(BF16)
            total += nn_dot(analysis_v[:, j : j + 256], hot)
        odd = iota((WAVES, 2 * LANES), 0) & 1
        total = jnp.where((odd * south) == 1, -total, total)
        sorted_s[:, pl.ds(pl.multiple_of(pair * 256, 256), 256)] = total.astype(BF16)

    local[4].wait()
    syn_f[...] = synthesis_v[...].astype(F32)
    for ri in range(ROWS_DEV):
        syn_s[:, ri * LANES : (ri + 1) * LANES] = syn_f[pl.ds(ri, NGX, stride=ROWS_DEV), :].astype(BF16)

    wait_all(recv1, recv_sem.at[0])
    spread_s[...] = recv1.reshape(2 * NGX, LANES)[...].astype(F32)
    head = spread_s[pl.ds(0, NGX, stride=2), :].T
    tail = spread_s[pl.ds(1, NGX, stride=2), :].T
    loops = jnp.concatenate([head, tail], axis=0)
    loops = jnp.concatenate([loops[8 * s : 8 * s + 8] for s in range(LOOPS_DEV)], axis=1)
    spec = nt_dot(loops.astype(BF16), sorted_s[...])
    spec = jnp.where(iota((8, WAVES), 1) < WAVES - own, spec, 0.0).astype(BF16).astype(F32)
    wide = jnp.broadcast_to(spec[:, None, :], (8, ROWS_DEV, WAVES)).reshape(8 * ROWS_DEV, WAVES)
    ri = iota((8 * ROWS_DEV, WAVES), 0) & (ROWS_DEV - 1)
    wide = jnp.concatenate([jnp.where(ri == r, wide, 0.0) for r in range(ROWS_DEV)], axis=1)
    wide = jnp.concatenate([wide, jnp.zeros_like(wide)], axis=0).astype(BF16)
    send2[...] = nt_dot(syn_s[...], wide).astype(BF16).astype(F32)

    exchange(lambda to: send2.at[pl.ds(to, 1)], lambda to: recv2.at[pl.ds(to, 1)], 1)
    wave_s[...] = jnp.broadcast_to(wave.astype(F32), (WAVES, WAVES)).T.astype(I32) + FIRST_WAVE
    lon_start = x * LON_DEV

    @pl.loop(0, NGX // 16)
    def _(i):
        at = pl.ds(pl.multiple_of(i * 16, 16), 16)
        col = wave_s[at, :]
        for n in range(0, LON_PAD, LANES):
            lon = iota((16, LANES), 1) + (lon_start + n)
            cos, sin = table_tile(col, lon)
            table_s[0, at, n : n + LANES] = cos
            table_s[1, at, n : n + LANES] = sin

    local[5].wait()
    local[6].wait()

    wait_all(recv2, recv_sem.at[1])
    send3[...] = recv2[...].T[: 8 * ROWS_DEV].astype(BF16)
    for d in (2, 1, 3):
        pltpu.make_async_remote_copy(
            src_ref=send3,
            dst_ref=recv3.at[x],
            send_sem=send_sem.at[2],
            recv_sem=recv_sem.at[2],
            device_id=((x + d) & (NX - 1), gx),
            device_id_type=MESH,
        ).start()
    pltpu.make_async_copy(send3, recv3.at[x], recv_sem.at[2]).start()

    wait_all(recv3, recv_sem.at[2])
    half = 4 * ROWS_DEV
    rows = jnp.concatenate(
        [jnp.concatenate([recv3[v, :half], recv3[v, half:]], axis=1) for v in range(NX)], axis=0
    )
    field = nn_dot(rows, table_s[...].reshape(2 * NGX, LON_PAD))
    field_s[...] = field.reshape(LEV, ROWS_DEV, LON_PAD)

    for n in range(0, LON_DEV, LANES):
        at = slice(n, min(n + LANES, LON_DEV))
        levels = [field_s[v, :, at] for v in range(LEV)]

        @pl.loop(0, POUT)
        def _(p):
            below = bracket_v[p, :, at]
            weight = frac_v[p, :, at]
            low, high = levels, levels[1:] + levels[-1:]
            for bit in range(4):
                mask = ((below >> bit) & 1) == 1
                low = [jnp.where(mask, b, a) for a, b in zip(low[0::2], low[1::2])]
                high = [jnp.where(mask, b, a) for a, b in zip(high[0::2], high[1::2])]
            out_ref[p, :, at] = (1.0 - weight) * low[0] + weight * high[0]

    wait_all(send1.at[pl.ds(0, NGX - 1)], send_sem.at[0])
    wait_all(send2.at[pl.ds(0, NGX - 1)], send_sem.at[1])
    wait_all(recv3.at[pl.ds(0, NX - 1)], send_sem.at[2])


def shards(fourier, lat_of_row, wave_order, analysis, synthesis, bracket, frac):
    lat = lat_of_row.reshape(LOOPS_DEV, LANES)
    wave = wave_order.reshape(1, WAVES)
    fourier = jnp.transpose(fourier, (1, 3, 2, 0))
    vmem = pl.BlockSpec(memory_space=pltpu.VMEM)
    hbm = pl.BlockSpec(memory_space=pltpu.HBM)
    return pl.pallas_call(
        kernel,
        out_shape=jax.ShapeDtypeStruct((POUT, ROWS_DEV, LON_DEV), F32),
        in_specs=[hbm] * 7,
        out_specs=vmem,
        scratch_shapes=[
            pltpu.VMEM((2, LOOPS_DEV, LEV_DEV, WAVES), BF16),
            pltpu.VMEM((1, WAVES), I32),
            pltpu.VMEM((LOOPS_DEV, LANES), I32),
            pltpu.VMEM((WAVES, HALF), BF16),
            pltpu.VMEM((NGX * ROWS_DEV, WAVES), BF16),
            pltpu.VMEM((POUT, ROWS_DEV, LON_DEV), I32),
            pltpu.VMEM((POUT, ROWS_DEV, LON_DEV), F32),
            pltpu.VMEM((NGX, 2, LANES), BF16),
            pltpu.VMEM((NGX, 2, LANES), BF16),
            pltpu.VMEM((NGX, LANES), F32),
            pltpu.VMEM((NGX, LANES), F32),
            pltpu.VMEM((8 * ROWS_DEV, NGX), BF16),
            pltpu.VMEM((NX, 8 * ROWS_DEV, NGX), BF16),
            pltpu.VMEM((2, 24, LANES), I32),
            pltpu.VMEM((WAVES, NLAT), BF16),
            pltpu.VMEM((2 * NGX, LANES), F32),
            pltpu.VMEM((NGX * ROWS_DEV, WAVES), F32),
            pltpu.VMEM((NGX, ROWS_DEV * WAVES), BF16),
            pltpu.VMEM((WAVES, LANES), I32),
            pltpu.VMEM((2, NGX, LON_PAD), BF16),
            pltpu.VMEM((LEV, ROWS_DEV, LON_PAD), F32),
            pltpu.SemaphoreType.DMA((7,)),
            pltpu.SemaphoreType.DMA((3,)),
            pltpu.SemaphoreType.DMA((3,)),
        ],
        compiler_params=pltpu.CompilerParams(
            collective_id=0, has_side_effects=True, vmem_limit_bytes=56 * 1024 * 1024
        ),
        cost_estimate=pl.CostEstimate(flops=10**9, bytes_accessed=1400000, transcendentals=0),
    )(
        fourier, wave, lat, analysis.reshape(WAVES, HALF),
        synthesis.reshape(NGX * ROWS_DEV, WAVES), bracket, frac,
    )


def solution(mesh):
    placed = (
        P(None, None, "grp", "gx"),
        P(),
        P(),
        P("gx", None, None),
        P("gx", None, None),
        P(None, "gx", "grp"),
        P(None, "gx", "grp"),
    )
    return jax.shard_map(
        shards, mesh=mesh, in_specs=placed, out_specs=P(None, "gx", "grp"), check_vma=False
    )
```

time: 52 us -> 42.6 us (0.82)
  local copies, waits for them, and re-layouts: 6.66 us -> 1.67 us
  Pallas kernels: 45 us -> 40.8 us
    unnamed x15 -> x1, local copies, waits for them, and re-layouts: 6.66 us -> 1.67 us
    pallas_call x1, Pallas kernels: 45 us -> 40.8 us  [shards(): pl.pallas_call(kernel, out_shape=jax.ShapeDtypeStruct((POUT, ROWS_DEV, LO...]
where the time goes in v2:
time: 42.6 us; the launch traced here: 42.5 us
  Pallas kernels  40.8 us (96%)
  local copies, waits for them, and re-layouts  1.67 us (4%)
    pallas_call x1, Pallas kernels, shards(): pl.pallas_call(kernel, out_shape=jax.ShapeDtypeStruct((POUT, ROWS_DEV, LO...  40.8 us
    unnamed x1, local copies, waits for them, and re-layouts  1.67 us

profile of v2, /device:TPU:1, one launch (start us, length us, event | category | flops | bytes accessed | tf_op | source)
XLA Modules:
  0.0 42.5 jit_solution(2973010935104925285)
XLA Ops:
  0.0 40.8 %shard_map.73 = f32[8,8,900]{2,1,0:T(8,128)} custom-call(bf16[2,20,4,128]{3,2,1,0:T(4,128)(2,1)} %bitcast.7, s32[1,128]{1,0:T(1,128)} %bitcast.9, s32[20,128]{1,0:T(8,128)} %bitcast.8, bf16[128,1280]{1,0:T(8,128)(2,1)} %bitcast.5, bf16[1024,128]{1,0:T(8,128)(2,1)} %bitcast.6, s32[8,8,900]{2,1,0:T(8,128)} %bracket_ref.1, f32[8,8,900]{2,1,0:T(8,128)} %frac_ref.1), custom_call_target="tpu_custom_call" | custom-call | flops 1000000000 | bytes 1400000 | tf_op jit(solution)/shard_map/pallas_call | solution.py:257
  40.8 1.7 %copy.9 = f32[8,8,900]{2,1,0:T(8,128)} copy(f32[8,8,900]{2,1,0:T(8,128)} %shard_map.73) | data formatting | bytes 460800

commit v3 on v2

--- a/solution.py
+++ b/solution.py
@@ -256,7 +256,7 @@
     hbm = pl.BlockSpec(memory_space=pltpu.HBM)
     return pl.pallas_call(
         kernel,
-        out_shape=jax.ShapeDtypeStruct((POUT, ROWS_DEV, LON_DEV), F32),
+        out_shape=pltpu.VMEM((POUT, ROWS_DEV, LON_DEV), F32),
         in_specs=[hbm] * 7,
         out_specs=vmem,
         scratch_shapes=[

time: 42.6 us -> 40.9 us (0.960)
  local copies, waits for them, and re-layouts: 1.67 us -> 0.71 us
  Pallas kernels: 40.8 us -> 40.1 us
    unnamed x1, local copies, waits for them, and re-layouts: 1.67 us -> 0.71 us
    pallas_call x1, Pallas kernels: 40.8 us -> 40.1 us  [shards(): pl.pallas_call(kernel, out_shape=pltpu.VMEM((POUT, ROWS_DEV, LON_DEV), F3...]
where the time goes in v3:
time: 40.9 us; the launch traced here: 40.8 us
  Pallas kernels  40.1 us (98%)
  local copies, waits for them, and re-layouts  0.71 us (2%)
    pallas_call x1, Pallas kernels, shards(): pl.pallas_call(kernel, out_shape=pltpu.VMEM((POUT, ROWS_DEV, LON_DEV), F3...  40.1 us

profile of v3, /device:TPU:1, one launch (start us, length us, event | category | flops | bytes accessed | tf_op | source)
XLA Modules:
  0.0 40.8 jit_solution(9180321463219776481)
XLA Ops:
  0.0 40.1 %shard_map.73 = f32[8,8,900]{2,1,0:T(8,128)S(1)} custom-call(bf16[2,20,4,128]{3,2,1,0:T(4,128)(2,1)} %bitcast.7, s32[1,128]{1,0:T(1,128)} %bitcast.9, s32[20,128]{1,0:T(8,128)} %bitcast.8, bf16[128,1280]{1,0:T(8,128)(2,1)} %bitcast.5, bf16[1024,128]{1,0:T(8,128)(2,1)} %bitcast.6, s32[8,8,900]{2,1,0:T(8,128)} %bracket_ref.1, f32[8,8,900]{2,1,0:T(8,128)} %frac_ref.1), custom_call_target="tpu_custom_call" | custom-call | flops 1000000000 | bytes 1400000 | tf_op jit(solution)/shard_map/pallas_call | solution.py:257
  40.1 0.7 %copy.9 = f32[8,8,900]{2,1,0:T(8,128)} copy(f32[8,8,900]{2,1,0:T(8,128)S(1)} %shard_map.73) | data formatting | bytes 460800

commit v4 on v3

--- a/solution.py
+++ b/solution.py
@@ -66,6 +66,25 @@
     cos = jnp.where(((quarter + 1) & 2) == 2, -2.0 * cos, 2.0 * cos)
     sin = jnp.where((quarter & 2) == 2, 2.0 * sin, -2.0 * sin)
     return cos.astype(BF16), sin.astype(BF16)
+
+
+def one_level(levels, bits):
+    for bit in bits:
+        levels = [jnp.where(bit, b, a) for a, b in zip(levels[0::2], levels[1::2])]
+    return levels[0]
+
+
+def two_levels(levels, below):
+    bits = [(below & (1 << i)) != 0 for i in range(4)]
+
+    def pair(values, bits):
+        if not bits:
+            return values[0], values[1]
+        even, after = pair(values[0::2], bits[1:])
+        odd = one_level(values[1::2], bits[1:])
+        return jnp.where(bits[0], odd, even), jnp.where(bits[0], after, odd)
+
+    return pair(levels + levels[-1:], bits)
 
 
 def farthest_first(step, half):
@@ -225,23 +244,17 @@
     rows = jnp.concatenate(
         [jnp.concatenate([recv3[v, :half], recv3[v, half:]], axis=1) for v in range(NX)], axis=0
     )
-    field = nn_dot(rows, table_s[...].reshape(2 * NGX, LON_PAD))
-    field_s[...] = field.reshape(LEV, ROWS_DEV, LON_PAD)
-
-    for n in range(0, LON_DEV, LANES):
-        at = slice(n, min(n + LANES, LON_DEV))
-        levels = [field_s[v, :, at] for v in range(LEV)]
-
-        @pl.loop(0, POUT)
-        def _(p):
-            below = bracket_v[p, :, at]
-            weight = frac_v[p, :, at]
-            low, high = levels, levels[1:] + levels[-1:]
-            for bit in range(4):
-                mask = ((below >> bit) & 1) == 1
-                low = [jnp.where(mask, b, a) for a, b in zip(low[0::2], low[1::2])]
-                high = [jnp.where(mask, b, a) for a, b in zip(high[0::2], high[1::2])]
-            out_ref[p, :, at] = (1.0 - weight) * low[0] + weight * high[0]
+    for n in range(0, LON_DEV, 2 * LANES):
+        table = table_s[:, :, n : n + 2 * LANES].reshape(2 * NGX, 2 * LANES)
+        field = nn_dot(rows, table).reshape(LEV, ROWS_DEV, 2 * LANES)
+        for k in range(n, min(n + 2 * LANES, LON_DEV), LANES):
+            width = min(LANES, LON_DEV - k)
+            levels = [field[v, :, k - n : k - n + width] for v in range(LEV)]
+            for p in range(POUT):
+                below = bracket_v[p, :, k : k + width]
+                weight = frac_v[p, :, k : k + width]
+                low, high = two_levels(levels, below)
+                out_ref[p, :, k : k + width] = (1.0 - weight) * low + weight * high
 
     wait_all(send1.at[pl.ds(0, NGX - 1)], send_sem.at[0])
     wait_all(send2.at[pl.ds(0, NGX - 1)], send_sem.at[1])

time: 40.9 us -> 40.5 us (level)
  Pallas kernels: 40.1 us -> 39.6 us
    pallas_call x1, Pallas kernels: 40.1 us -> 39.6 us  [shards(): pl.pallas_call(kernel, out_shape=pltpu.VMEM((POUT, ROWS_DEV, LON_DEV), F3...]
where the time goes in v4:
time: 40.5 us; the launch traced here: 40.3 us
  Pallas kernels  39.6 us (98%)
  local copies, waits for them, and re-layouts  0.71 us (2%)
    pallas_call x1, Pallas kernels, shards(): pl.pallas_call(kernel, out_shape=pltpu.VMEM((POUT, ROWS_DEV, LON_DEV), F3...  39.6 us

profile of v4, /device:TPU:1, one launch (start us, length us, event | category | flops | bytes accessed | tf_op | source)
XLA Modules:
  0.0 40.3 jit_solution(13584883647309544882)
XLA Ops:
  0.0 39.6 %shard_map.73 = f32[8,8,900]{2,1,0:T(8,128)S(1)} custom-call(bf16[2,20,4,128]{3,2,1,0:T(4,128)(2,1)} %bitcast.7, s32[1,128]{1,0:T(1,128)} %bitcast.9, s32[20,128]{1,0:T(8,128)} %bitcast.8, bf16[128,1280]{1,0:T(8,128)(2,1)} %bitcast.5, bf16[1024,128]{1,0:T(8,128)(2,1)} %bitcast.6, s32[8,8,900]{2,1,0:T(8,128)} %bracket_ref.1, f32[8,8,900]{2,1,0:T(8,128)} %frac_ref.1), custom_call_target="tpu_custom_call" | custom-call | flops 1000000000 | bytes 1400000 | tf_op jit(solution)/shard_map/pallas_call | solution.py:270
  39.6 0.7 %copy.9 = f32[8,8,900]{2,1,0:T(8,128)} copy(f32[8,8,900]{2,1,0:T(8,128)S(1)} %shard_map.73) | data formatting | bytes 460800

commit v5 on v4

--- a/solution.py
+++ b/solution.py
@@ -20,6 +20,8 @@
 HALF = NLAT // 2
 LANES = 128
 LON_PAD = 1024
+EARLY = 1
+FAR = 3
 
 
 def iota(shape, axis):
@@ -95,7 +97,7 @@
     fourier_ref, wave_ref, lat_ref, analysis_ref, synthesis_ref, bracket_ref, frac_ref,
     out_ref,
     fourier_v, wave_v, lat_v, analysis_v, synthesis_v, bracket_v, frac_v,
-    send1, recv1, send2, recv2, send3, recv3,
+    send1, recv1, send2, recv2, send3, recv3, far2, rows_s,
     lats_s, sorted_s, spread_s, syn_f, syn_s, wave_s, table_s, field_s,
     local_sem, send_sem, recv_sem,
 ):
@@ -103,16 +105,23 @@
     gx = lax.axis_index("gx")
     z, yc = gx >> 3, gx & (NYC - 1)
 
+    def near(tz, count, action):
+        for j in range(count):
+            action((tz << 3) + ((yc + farthest_first(j, NYC // 2)) & (NYC - 1)))
+
     def peers(action):
-        def near(tz, count):
-            for j in range(count):
-                action((tz << 3) + ((yc + farthest_first(j, NYC // 2)) & (NYC - 1)))
-
         @pl.loop(0, NZ - 1)
         def _(k):
-            near((z + farthest_first(k, NZ // 2)) & (NZ - 1), NYC)
-
-        near(z, NYC - 1)
+            near((z + farthest_first(k, NZ // 2)) & (NZ - 1), NYC, action)
+
+        near(z, NYC - 1, action)
+
+    early = z < EARLY
+
+    @pl.when(early)
+    def _():
+        recv2[...] = jnp.zeros((NGX, LANES), F32)
+        far2[...] = jnp.zeros((NX, NGX, LANES), F32)
 
     barrier = pltpu.get_barrier_semaphore()
 
@@ -140,19 +149,15 @@
     for copy in local:
         copy.start()
 
-    def exchange(send, recv, stage):
-        def one(to):
-            pltpu.make_async_remote_copy(
-                src_ref=send(to),
-                dst_ref=recv(gx),
-                send_sem=send_sem.at[stage],
-                recv_sem=recv_sem.at[stage],
-                device_id=(x, to),
-                device_id_type=MESH,
-            ).start()
-
-        peers(one)
-        pltpu.make_async_copy(send(gx), recv(gx), recv_sem.at[stage]).start()
+    def push(src, dst, stage, tx, to):
+        pltpu.make_async_remote_copy(
+            src_ref=src,
+            dst_ref=dst,
+            send_sem=send_sem.at[stage],
+            recv_sem=recv_sem.at[stage],
+            device_id=(tx, to),
+            device_id_type=MESH,
+        ).start()
 
     def wait_all(ref, sem):
         pltpu.make_async_copy(ref, ref, sem).wait()
@@ -165,7 +170,8 @@
     spread_s[pl.ds(1, NGX, stride=2), :] = ordered[:, LANES:]
     send1.reshape(2 * NGX, LANES)[...] = spread_s[...].astype(BF16)
     pl.semaphore_wait(barrier, NGX - 1 + NX - 1)
-    exchange(lambda to: send1.at[to], lambda to: recv1.at[to], 0)
+    peers(lambda to: push(send1.at[to], recv1.at[gx], 0, x, to))
+    pltpu.make_async_copy(send1.at[gx], recv1.at[gx], recv_sem.at[0]).start()
 
     local[2].wait()
     lats = loop_lats(lat_v[...])
@@ -188,7 +194,7 @@
             total += nn_dot(analysis_v[:, j : j + 256], hot)
         odd = iota((WAVES, 2 * LANES), 0) & 1
         total = jnp.where((odd * south) == 1, -total, total)
-        sorted_s[:, pl.ds(pl.multiple_of(pair * 256, 256), 256)] = total.astype(BF16)
+        sorted_s[pl.ds(pl.multiple_of(pair * 256, 256), 256), :] = total.T.astype(BF16)
 
     local[4].wait()
     syn_f[...] = synthesis_v[...].astype(F32)
@@ -201,15 +207,42 @@
     tail = spread_s[pl.ds(1, NGX, stride=2), :].T
     loops = jnp.concatenate([head, tail], axis=0)
     loops = jnp.concatenate([loops[8 * s : 8 * s + 8] for s in range(LOOPS_DEV)], axis=1)
-    spec = nt_dot(loops.astype(BF16), sorted_s[...])
+    spec = nn_dot(loops.astype(BF16), sorted_s[...])
     spec = jnp.where(iota((8, WAVES), 1) < WAVES - own, spec, 0.0).astype(BF16).astype(F32)
     wide = jnp.broadcast_to(spec[:, None, :], (8, ROWS_DEV, WAVES)).reshape(8 * ROWS_DEV, WAVES)
     ri = iota((8 * ROWS_DEV, WAVES), 0) & (ROWS_DEV - 1)
     wide = jnp.concatenate([jnp.where(ri == r, wide, 0.0) for r in range(ROWS_DEV)], axis=1)
-    wide = jnp.concatenate([wide, jnp.zeros_like(wide)], axis=0).astype(BF16)
+    wide = jnp.concatenate([wide, wide], axis=0).astype(BF16)
     send2[...] = nt_dot(syn_s[...], wide).astype(BF16).astype(F32)
 
-    exchange(lambda to: send2.at[pl.ds(to, 1)], lambda to: recv2.at[pl.ds(to, 1)], 1)
+    def row_of(to):
+        return send2.at[pl.ds(to, 1)]
+
+    def push_row(to):
+        push(row_of(to), recv2.at[pl.ds(gx, 1)], 1, x, to)
+
+    def push_far(to):
+        for d in (2, 1, 3, 0):
+            push(row_of(to), far2.at[x, pl.ds(gx, 1)], 3, (x + d) & (NX - 1), to)
+
+    @pl.loop(0, FAR)
+    def _(k):
+        tz = (z + farthest_first(k, NZ // 2)) & (NZ - 1)
+
+        @pl.when(tz < EARLY)
+        def _():
+            near(tz, NYC, push_far)
+
+        @pl.when(tz >= EARLY)
+        def _():
+            near(tz, NYC, push_row)
+
+    @pl.loop(FAR, NZ - 1)
+    def _(k):
+        near((z + farthest_first(k, NZ // 2)) & (NZ - 1), NYC, push_row)
+
+    near(z, NYC - 1, push_row)
+    pltpu.make_async_copy(row_of(gx), recv2.at[pl.ds(gx, 1)], recv_sem.at[1]).start()
     wave_s[...] = jnp.broadcast_to(wave.astype(F32), (WAVES, WAVES)).T.astype(I32) + FIRST_WAVE
     lon_start = x * LON_DEV
 
@@ -226,24 +259,43 @@
     local[5].wait()
     local[6].wait()
 
-    wait_all(recv2, recv_sem.at[1])
-    send3[...] = recv2[...].T[: 8 * ROWS_DEV].astype(BF16)
+    @pl.when(early)
+    def _():
+        wait_all(recv2.at[pl.ds(0, (NZ - FAR) * NYC)], recv_sem.at[1])
+
+    @pl.when(jnp.logical_not(early))
+    def _():
+        wait_all(recv2, recv_sem.at[1])
+
+    half = 4 * ROWS_DEV
+    send3[...] = recv2[...].T[: 2 * half].astype(BF16)
     for d in (2, 1, 3):
-        pltpu.make_async_remote_copy(
-            src_ref=send3,
-            dst_ref=recv3.at[x],
-            send_sem=send_sem.at[2],
-            recv_sem=recv_sem.at[2],
-            device_id=((x + d) & (NX - 1), gx),
-            device_id_type=MESH,
-        ).start()
+        push(send3, recv3.at[x], 2, (x + d) & (NX - 1), gx)
     pltpu.make_async_copy(send3, recv3.at[x], recv_sem.at[2]).start()
 
-    wait_all(recv3, recv_sem.at[2])
-    half = 4 * ROWS_DEV
-    rows = jnp.concatenate(
-        [jnp.concatenate([recv3[v, :half], recv3[v, half:]], axis=1) for v in range(NX)], axis=0
-    )
+    def set_rows(v, block):
+        at = slice(v * half, (v + 1) * half)
+        rows_s[at, :NGX] = block[:half]
+        rows_s[at, NGX:] = block[half:]
+
+    @pl.when(early)
+    def _():
+        wait_all(far2.at[:, pl.ds(0, FAR * NYC)], recv_sem.at[3])
+        wait_all(recv3, recv_sem.at[2])
+        first = iota((NGX, LANES), 1) < 2 * half
+        for v in range(0, NX, 2):
+            both = jnp.where(first, far2[v], far2[v + 1]).T
+            for i in range(2):
+                far = both[2 * half * i : 2 * half * (i + 1)]
+                set_rows(v + i, (recv3[v + i].astype(F32) + far).astype(BF16))
+
+    @pl.when(jnp.logical_not(early))
+    def _():
+        wait_all(recv3, recv_sem.at[2])
+        for v in range(NX):
+            set_rows(v, recv3[v])
+
+    rows = rows_s[...]
     for n in range(0, LON_DEV, 2 * LANES):
         table = table_s[:, :, n : n + 2 * LANES].reshape(2 * NGX, 2 * LANES)
         field = nn_dot(rows, table).reshape(LEV, ROWS_DEV, 2 * LANES)
@@ -257,7 +309,19 @@
                 out_ref[p, :, k : k + width] = (1.0 - weight) * low + weight * high
 
     wait_all(send1.at[pl.ds(0, NGX - 1)], send_sem.at[0])
-    wait_all(send2.at[pl.ds(0, NGX - 1)], send_sem.at[1])
+    wait_all(send2.at[pl.ds(0, NGX - 1 - NYC * EARLY)], send_sem.at[1])
+    for tz in range(EARLY):
+        away = (tz - z) & (NZ - 1)
+        is_far = jnp.abs(away - NZ // 2) <= FAR // 2
+
+        @pl.when(is_far)
+        def _():
+            wait_all(far2.at[0, pl.ds(0, NX * NYC)], send_sem.at[3])
+
+        @pl.when(jnp.logical_not(is_far))
+        def _():
+            wait_all(send2.at[pl.ds(0, NYC)], send_sem.at[1])
+
     wait_all(recv3.at[pl.ds(0, NX - 1)], send_sem.at[2])
 
 
@@ -286,8 +350,10 @@
             pltpu.VMEM((NGX, LANES), F32),
             pltpu.VMEM((8 * ROWS_DEV, NGX), BF16),
             pltpu.VMEM((NX, 8 * ROWS_DEV, NGX), BF16),
+            pltpu.VMEM((NX, NGX, LANES), F32),
+            pltpu.VMEM((LEV * ROWS_DEV, 2 * NGX), BF16),
             pltpu.VMEM((2, 24, LANES), I32),
-            pltpu.VMEM((WAVES, NLAT), BF16),
+            pltpu.VMEM((NLAT, WAVES), BF16),
             pltpu.VMEM((2 * NGX, LANES), F32),
             pltpu.VMEM((NGX * ROWS_DEV, WAVES), F32),
             pltpu.VMEM((NGX, ROWS_DEV * WAVES), BF16),
@@ -295,8 +361,8 @@
             pltpu.VMEM((2, NGX, LON_PAD), BF16),
             pltpu.VMEM((LEV, ROWS_DEV, LON_PAD), F32),
             pltpu.SemaphoreType.DMA((7,)),
-            pltpu.SemaphoreType.DMA((3,)),
-            pltpu.SemaphoreType.DMA((3,)),
+            pltpu.SemaphoreType.DMA((4,)),
+            pltpu.SemaphoreType.DMA((4,)),
         ],
         compiler_params=pltpu.CompilerParams(
             collective_id=0, has_side_effects=True, vmem_limit_bytes=56 * 1024 * 1024

time: 40.5 us -> 39.7 us (0.980)
  Pallas kernels: 39.6 us -> 38.8 us
    pallas_call x1, Pallas kernels: 39.6 us -> 38.8 us  [shards(): pl.pallas_call(kernel, out_shape=pltpu.VMEM((POUT, ROWS_DEV, LON_DEV), F3...]
where the time goes in v5:
time: 39.7 us; the launch traced here: 39.5 us
  Pallas kernels  38.8 us (98%)
  local copies, waits for them, and re-layouts  0.71 us (2%)
    pallas_call x1, Pallas kernels, shards(): pl.pallas_call(kernel, out_shape=pltpu.VMEM((POUT, ROWS_DEV, LON_DEV), F3...  38.8 us

profile of v5, /device:TPU:1, one launch (start us, length us, event | category | flops | bytes accessed | tf_op | source)
XLA Modules:
  0.0 39.5 jit_solution(4964648268553974959)
XLA Ops:
  0.0 38.8 %shard_map.73 = f32[8,8,900]{2,1,0:T(8,128)S(1)} custom-call(bf16[2,20,4,128]{3,2,1,0:T(4,128)(2,1)} %bitcast.7, s32[1,128]{1,0:T(1,128)} %bitcast.9, s32[20,128]{1,0:T(8,128)} %bitcast.8, bf16[128,1280]{1,0:T(8,128)(2,1)} %bitcast.5, bf16[1024,128]{1,0:T(8,128)(2,1)} %bitcast.6, s32[8,8,900]{2,1,0:T(8,128)} %bracket_ref.1, f32[8,8,900]{2,1,0:T(8,128)} %frac_ref.1), custom_call_target="tpu_custom_call" | custom-call | flops 1000000000 | bytes 1400000 | tf_op jit(solution)/shard_map/pallas_call | solution.py:334
  38.8 0.7 %copy.9 = f32[8,8,900]{2,1,0:T(8,128)} copy(f32[8,8,900]{2,1,0:T(8,128)S(1)} %shard_map.73) | data formatting | bytes 460800

commit v6 on v5

--- a/solution.py
+++ b/solution.py
@@ -20,8 +20,10 @@
 HALF = NLAT // 2
 LANES = 128
 LON_PAD = 1024
-EARLY = 1
-FAR = 3
+FIRST = 4
+TABLE_SOON = 5
+EARLY = 3
+FAR = 5
 
 
 def iota(shape, axis):
@@ -225,29 +227,23 @@
         for d in (2, 1, 3, 0):
             push(row_of(to), far2.at[x, pl.ds(gx, 1)], 3, (x + d) & (NX - 1), to)
 
-    @pl.loop(0, FAR)
-    def _(k):
-        tz = (z + farthest_first(k, NZ // 2)) & (NZ - 1)
-
-        @pl.when(tz < EARLY)
+    def push_plane(tz):
+        is_far = jnp.abs(((tz - z) & (NZ - 1)) - NZ // 2) <= FAR // 2
+        at_once = jnp.logical_and(is_far, tz < EARLY)
+
+        @pl.when(at_once)
         def _():
             near(tz, NYC, push_far)
 
-        @pl.when(tz >= EARLY)
+        @pl.when(jnp.logical_and(jnp.logical_not(at_once), tz != z))
         def _():
             near(tz, NYC, push_row)
 
-    @pl.loop(FAR, NZ - 1)
-    def _(k):
-        near((z + farthest_first(k, NZ // 2)) & (NZ - 1), NYC, push_row)
-
-    near(z, NYC - 1, push_row)
-    pltpu.make_async_copy(row_of(gx), recv2.at[pl.ds(gx, 1)], recv_sem.at[1]).start()
+    pl.loop(0, FIRST)(push_plane)
     wave_s[...] = jnp.broadcast_to(wave.astype(F32), (WAVES, WAVES)).T.astype(I32) + FIRST_WAVE
     lon_start = x * LON_DEV
 
-    @pl.loop(0, NGX // 16)
-    def _(i):
+    def table_rows(i):
         at = pl.ds(pl.multiple_of(i * 16, 16), 16)
         col = wave_s[at, :]
         for n in range(0, LON_PAD, LANES):
@@ -256,6 +252,11 @@
             table_s[0, at, n : n + LANES] = cos
             table_s[1, at, n : n + LANES] = sin
 
+    pl.loop(0, TABLE_SOON)(table_rows)
+    pl.loop(FIRST, NZ)(push_plane)
+    near(z, NYC - 1, push_row)
+    pltpu.make_async_copy(row_of(gx), recv2.at[pl.ds(gx, 1)], recv_sem.at[1]).start()
+    pl.loop(TABLE_SOON, NGX // 16)(table_rows)
     local[5].wait()
     local[6].wait()
 

time: 39.7 us -> 39.3 us (0.990)
  Pallas kernels: 38.8 us -> 38.4 us
where the time goes in v6:
time: 39.3 us; the launch traced here: 39.2 us
  Pallas kernels  38.4 us (98%)
  local copies, waits for them, and re-layouts  0.71 us (2%)
    pallas_call x1, Pallas kernels, shards(): pl.pallas_call(kernel, out_shape=pltpu.VMEM((POUT, ROWS_DEV, LON_DEV), F3...  38.4 us

profile of v6, /device:TPU:1, one launch (start us, length us, event | category | flops | bytes accessed | tf_op | source)
XLA Modules:
  0.0 39.2 jit_solution(955485672742035266)
XLA Ops:
  0.0 38.4 %shard_map.73 = f32[8,8,900]{2,1,0:T(8,128)S(1)} custom-call(bf16[2,20,4,128]{3,2,1,0:T(4,128)(2,1)} %bitcast.7, s32[1,128]{1,0:T(1,128)} %bitcast.9, s32[20,128]{1,0:T(8,128)} %bitcast.8, bf16[128,1280]{1,0:T(8,128)(2,1)} %bitcast.5, bf16[1024,128]{1,0:T(8,128)(2,1)} %bitcast.6, s32[8,8,900]{2,1,0:T(8,128)} %bracket_ref.1, f32[8,8,900]{2,1,0:T(8,128)} %frac_ref.1), custom_call_target="tpu_custom_call" | custom-call | flops 1000000000 | bytes 1400000 | tf_op jit(solution)/shard_map/pallas_call | solution.py:335
  38.5 0.7 %copy.9 = f32[8,8,900]{2,1,0:T(8,128)} copy(f32[8,8,900]{2,1,0:T(8,128)S(1)} %shard_map.73) | data formatting | bytes 460800

commit v7 on v6

--- a/solution.py
+++ b/solution.py
@@ -99,7 +99,7 @@
     fourier_ref, wave_ref, lat_ref, analysis_ref, synthesis_ref, bracket_ref, frac_ref,
     out_ref,
     fourier_v, wave_v, lat_v, analysis_v, synthesis_v, bracket_v, frac_v,
-    send1, recv1, send2, recv2, send3, recv3, far2, rows_s,
+    send1, recv1, send2, recv2, send3, recv3, far2, far_s, rows_s,
     lats_s, sorted_s, spread_s, syn_f, syn_s, wave_s, table_s, field_s,
     local_sem, send_sem, recv_sem,
 ):
@@ -282,13 +282,14 @@
     @pl.when(early)
     def _():
         wait_all(far2.at[:, pl.ds(0, FAR * NYC)], recv_sem.at[3])
-        wait_all(recv3, recv_sem.at[2])
         first = iota((NGX, LANES), 1) < 2 * half
         for v in range(0, NX, 2):
             both = jnp.where(first, far2[v], far2[v + 1]).T
-            for i in range(2):
-                far = both[2 * half * i : 2 * half * (i + 1)]
-                set_rows(v + i, (recv3[v + i].astype(F32) + far).astype(BF16))
+            far_s[2 * half * v : 2 * half * (v + 2), :] = both
+        wait_all(recv3, recv_sem.at[2])
+        for v in range(NX):
+            far = far_s[2 * half * v : 2 * half * (v + 1), :]
+            set_rows(v, (recv3[v].astype(F32) + far).astype(BF16))
 
     @pl.when(jnp.logical_not(early))
     def _():
@@ -352,6 +353,7 @@
             pltpu.VMEM((8 * ROWS_DEV, NGX), BF16),
             pltpu.VMEM((NX, 8 * ROWS_DEV, NGX), BF16),
             pltpu.VMEM((NX, NGX, LANES), F32),
+            pltpu.VMEM((NX * 8 * ROWS_DEV, NGX), F32),
             pltpu.VMEM((LEV * ROWS_DEV, 2 * NGX), BF16),
             pltpu.VMEM((2, 24, LANES), I32),
             pltpu.VMEM((NLAT, WAVES), BF16),

time: 39.3 us -> 39.2 us (level)
  no operation moved by 1% of the time
where the time goes in v7:
time: 39.2 us; the launch traced here: 39.1 us
  Pallas kernels  38.4 us (98%)
  local copies, waits for them, and re-layouts  0.71 us (2%)
    pallas_call x1, Pallas kernels, shards(): pl.pallas_call(kernel, out_shape=pltpu.VMEM((POUT, ROWS_DEV, LON_DEV), F3...  38.4 us

profile of v7, /device:TPU:1, one launch (start us, length us, event | category | flops | bytes accessed | tf_op | source)
XLA Modules:
  0.0 39.1 jit_solution(18049838641615591364)
XLA Ops:
  0.0 38.4 %shard_map.73 = f32[8,8,900]{2,1,0:T(8,128)S(1)} custom-call(bf16[2,20,4,128]{3,2,1,0:T(4,128)(2,1)} %bitcast.7, s32[1,128]{1,0:T(1,128)} %bitcast.9, s32[20,128]{1,0:T(8,128)} %bitcast.8, bf16[128,1280]{1,0:T(8,128)(2,1)} %bitcast.5, bf16[1024,128]{1,0:T(8,128)(2,1)} %bitcast.6, s32[8,8,900]{2,1,0:T(8,128)} %bracket_ref.1, f32[8,8,900]{2,1,0:T(8,128)} %frac_ref.1), custom_call_target="tpu_custom_call" | custom-call | flops 1000000000 | bytes 1400000 | tf_op jit(solution)/shard_map/pallas_call | solution.py:336
  38.4 0.7 %copy.9 = f32[8,8,900]{2,1,0:T(8,128)} copy(f32[8,8,900]{2,1,0:T(8,128)S(1)} %shard_map.73) | data formatting | bytes 460800

commit v8 on v7

--- a/solution.py
+++ b/solution.py
@@ -223,9 +223,8 @@
     def push_row(to):
         push(row_of(to), recv2.at[pl.ds(gx, 1)], 1, x, to)
 
-    def push_far(to):
-        for d in (2, 1, 3, 0):
-            push(row_of(to), far2.at[x, pl.ds(gx, 1)], 3, (x + d) & (NX - 1), to)
+    def push_far(d, to):
+        push(row_of(to), far2.at[x, pl.ds(gx, 1)], 3, (x + d) & (NX - 1), to)
 
     def push_plane(tz):
         is_far = jnp.abs(((tz - z) & (NZ - 1)) - NZ // 2) <= FAR // 2
@@ -233,7 +232,8 @@
 
         @pl.when(at_once)
         def _():
-            near(tz, NYC, push_far)
+            for d in (2, 1, 3, 0):
+                near(tz, NYC, functools.partial(push_far, d))
 
         @pl.when(jnp.logical_and(jnp.logical_not(at_once), tz != z))
         def _():

time: 39.2 us -> 39.1 us (level)
  no operation moved by 1% of the time
where the time goes in v8:
time: 39.1 us; the launch traced here: 39 us
  Pallas kernels  38.3 us (98%)
  local copies, waits for them, and re-layouts  0.71 us (2%)
    pallas_call x1, Pallas kernels, shards(): pl.pallas_call(kernel, out_shape=pltpu.VMEM((POUT, ROWS_DEV, LON_DEV), F3...  38.3 us

profile of v8, /device:TPU:1, one launch (start us, length us, event | category | flops | bytes accessed | tf_op | source)
XLA Modules:
  0.0 39.0 jit_solution(10693766440883277073)
XLA Ops:
  0.0 38.3 %shard_map.73 = f32[8,8,900]{2,1,0:T(8,128)S(1)} custom-call(bf16[2,20,4,128]{3,2,1,0:T(4,128)(2,1)} %bitcast.7, s32[1,128]{1,0:T(1,128)} %bitcast.9, s32[20,128]{1,0:T(8,128)} %bitcast.8, bf16[128,1280]{1,0:T(8,128)(2,1)} %bitcast.5, bf16[1024,128]{1,0:T(8,128)(2,1)} %bitcast.6, s32[8,8,900]{2,1,0:T(8,128)} %bracket_ref.1, f32[8,8,900]{2,1,0:T(8,128)} %frac_ref.1), custom_call_target="tpu_custom_call" | custom-call | flops 1000000000 | bytes 1400000 | tf_op jit(solution)/shard_map/pallas_call | solution.py:336
  38.3 0.7 %copy.9 = f32[8,8,900]{2,1,0:T(8,128)} copy(f32[8,8,900]{2,1,0:T(8,128)S(1)} %shard_map.73) | data formatting | bytes 460800
